TPU v7x, 32 devices: a whole 2x2x4 slice. The times are simulated.
32 devices in a mesh: dp: 4 (over y, core), tensor: 8 (over z, x).
Axes of the slice: x: 2, y: 2, z: 4, core: 2. Of those that a mesh axis runs over, the one named last changes fastest.
Arguments:
- normed: bfloat16 [2304, 1536], P(('dp', 'tensor')), may hold values from -6 to 6
- out_grad: bfloat16 [2304, 1536], P(('dp', 'tensor')), may hold values from -6 to 6
- gate_weight: bfloat16 [1536, 8960], P(None, 'tensor'), may hold values from -0.15625 to 0.15625
- up_weight: bfloat16 [1536, 8960], P(None, 'tensor'), may hold values from -0.15625 to 0.15625
- down_weight: bfloat16 [8960, 1536], P('tensor'), may hold values from -0.0625 to 0.0625
Outputs:
- grad_input: bfloat16 [2304, 1536], P(('dp', 'tensor'))
- grad_gate: float32 [1536, 8960], P('dp', 'tensor')
- grad_up: float32 [1536, 8960], P('dp', 'tensor')
- grad_down: float32 [8960, 1536], P('tensor', 'dp')
All inputs are finite; a program needn't handle non-finite values.
Results may differ from a plain program's by a relative error of at most 0.0049.
Values may be sent and summed in bfloat16 or wider, within the bound.
A program may use at most 128 MiB of HBM per device.

v0:
```python
import jax
import jax.numpy as jnp
from jax import lax
from jax.sharding import PartitionSpec as P


def contract(left, right, left_dim, right_dim):
    return lax.dot_general(
        left, right, (((left_dim,), (right_dim,)), ((), ())), preferred_element_type=jnp.float32
    )


def on_device(normed, out_grad, gate_weight, up_weight, down_weight):
    replicas = lax.axis_size("dp")
    whole = lax.all_gather(normed, "tensor", axis=0, tiled=True)
    gate = jnp.dot(whole, gate_weight, preferred_element_type=jnp.float32)
    up = jnp.dot(whole, up_weight, preferred_element_type=jnp.float32)
    sig = jax.nn.sigmoid(gate)
    act = gate * sig
    hidden = (act * up).astype(jnp.bfloat16)
    piece = lax.all_gather(out_grad, "tensor", axis=0, tiled=True)
    part = contract(piece, down_weight, 1, 1)
    down_part = contract(hidden, piece, 0, 0)
    dgate = (part * up * sig * (1.0 + gate * (1.0 - sig))).astype(jnp.bfloat16)
    dup = (part * act).astype(jnp.bfloat16)
    grad_input = lax.psum_scatter(
        contract(dgate, gate_weight, 1, 1) + contract(dup, up_weight, 1, 1),
        "tensor",
        scatter_dimension=0,
        tiled=True,
    ).astype(jnp.bfloat16)
    paired = lax.psum_scatter(
        jnp.stack((contract(whole, dgate, 0, 0), contract(whole, dup, 0, 0)), 1),
        "dp",
        scatter_dimension=0,
        tiled=True,
    )
    grad_down = lax.psum_scatter(down_part, "dp", scatter_dimension=1, tiled=True)
    return (
        grad_input,
        paired[:, 0, :] / replicas,
        paired[:, 1, :] / replicas,
        grad_down / replicas,
    )


def solution(mesh):
    return jax.shard_map(
        on_device,
        mesh=mesh,
        in_specs=(
            P(("dp", "tensor"), None),
            P(("dp", "tensor"), None),
            P(None, "tensor"),
            P(None, "tensor"),
            P("tensor", None),
        ),
        out_specs=(
            P(("dp", "tensor"), None),
            P("dp", "tensor"),
            P("dp", "tensor"),
            P("tensor", "dp"),
        ),
        check_vma=False,
    )
```

profile of v0, /device:TPU:0, one launch (start us, length us, event | category | flops | bytes accessed | tf_op | source)
XLA Modules:
  0.0 383.2 jit_solution(18200272741636359240)
XLA Ops:
  7.2 0.7 all-gather.5.cloned.1.call-update
  8.0 0.7 all-gather.3.cloned.1.call-update
  8.7 50.1 %all-gather.5.cloned.1.call-done = bf16[576,1536]{1,0:T(8,128)(2,1)} async-done(((bf16[72,1536]{1,0:T(8,128)(2,1)}), bf16[576,1536]{1,0:T(8,128)(2,1)}) %all-gather.5.cloned.1.call-update) | async-done | bytes 1769488 | tf_op jit(solution)/shard_map/all_gather | solution.py:15
  58.9 5.6 %fusion.7 = f32[576,1120]{1,0:T(8,128)} fusion(bf16[576,1536]{1,0:T(8,128)(2,1)} %all-gather.5.cloned.1.call-done, bf16[1536,1120]{0,1:T(8,128)(2,1)S(1)} %copy-done), kind=kOutput, calls=%fused_computation.17 | convolution fusion | flops 1981808640 | bytes 7790592 | tf_op jit(solution)/shard_map/dot_general | solution.py:16
  64.5 4.0 %fusion.6 = f32[576,1120]{1,0:T(8,128)} fusion(bf16[576,1536]{1,0:T(8,128)(2,1)S(1)} %copy-done.4, bf16[1536,1120]{0,1:T(8,128)(2,1)S(1)} %copy-done.2), kind=kOutput, calls=%fused_computation.16 | convolution fusion | flops 1981808640 | bytes 7790592 | tf_op jit(solution)/shard_map/dot_general | solution.py:17
  68.5 37.5 %all-gather.3.cloned.1.call-done = bf16[576,1536]{1,0:T(8,128)(2,1)} async-done(((bf16[72,1536]{1,0:T(8,128)(2,1)}), bf16[576,1536]{1,0:T(8,128)(2,1)}) %all-gather.3.cloned.1.call-update) | async-done | bytes 1769488 | tf_op jit(solution)/shard_map/all_gather | solution.py:21
  106.0 7.1 %multiply_convert_fusion.1 = (bf16[576,1120]{1,0:T(8,128)(2,1)S(1)}, bf16[576,1120]{1,0:T(8,128)(2,1)S(1)}) fusion(f32[576,1120]{1,0:T(8,128)} %fusion.7, f32[576,1120]{1,0:T(8,128)} %fusion.6, bf16[576,1536]{1,0:T(8,128)(2,1)} %all-gather.3.cloned.1.call-done, bf16[1120,1536]{1,0:T(8,128)(2,1)} %param.9), kind=kOutput, calls=%fused_computation.5 | convolution fusion | flops 1990195200 | bytes 12951552 | tf_op jit(solution)/shard_map/dot_general | solution.py:8
  113.1 2.4 fusion.8
  115.6 0.5 copy-done.3
  116.0 4.3 %convolution_add_fusion = f32[576,1536]{1,0:T(8,128)} fusion(f32[576,1536]{1,0:T(8,128)S(1)} %fusion.8, bf16[576,1120]{1,0:T(8,128)(2,1)S(1)} %get-tuple-element.4, bf16[1536,1120]{0,1:T(8,128)(2,1)S(1)} %copy-done.3), kind=kOutput, calls=%fused_computation.3 | convolution fusion | flops 1982693376 | bytes 11808768 | tf_op jit(solution)/shard_map/dot_general | solution.py:8
  120.4 0.0 reduce-scatter.8.cloned.1.call-start
  120.5 1.4 copy-done.6
  121.9 8.1 %fusion.3 = f32[1120,1536]{1,0:T(8,128)} fusion(bf16[576,1536]{1,0:T(8,128)(2,1)S(1)} %copy-done.6, f32[576,1120]{1,0:T(8,128)} %fusion.6, f32[576,1120]{1,0:T(8,128)} %fusion.7), kind=kOutput, calls=%fused_computation.13 | convolution fusion | flops 1985679360 | bytes 13811712 | tf_op jit(solution)/shard_map/dot_general | solution.py:8
  130.0 0.2 reduce-scatter.6.cloned.1.call-start
  130.2 1.2 copy-done.5
  131.4 6.3 %convolution_bitcast_fusion = f32[1536,1,1120]{0,2,1:T(8,128)} fusion(bf16[576,1120]{1,0:T(8,128)(2,1)} %copy-done.9, bf16[576,1536]{1,0:T(8,128)(2,1)S(1)} %copy-done.5), kind=kOutput, calls=%fused_computation.1 | convolution fusion | flops 1981808640 | bytes 9940992 | tf_op jit(solution)/shard_map/dot_general | solution.py:8
  137.7 4.9 %convolution_bitcast_fusion.1 = f32[1536,1,1120]{0,2,1:T(8,128)} fusion(bf16[576,1120]{1,0:T(8,128)(2,1)S(1)} %copy-done.8, bf16[576,1536]{1,0:T(8,128)(2,1)S(1)} %copy-done.5), kind=kOutput, calls=%fused_computation.2 | convolution fusion | flops 1981808640 | bytes 9940992 | tf_op jit(solution)/shard_map/dot_general | solution.py:8
  142.6 11.6 %pad_maximum_fusion = f32[1536,2,1120]{0,2,1:T(8,128)} fusion(f32[1536,1,1120]{0,2,1:T(8,128)} %convolution_bitcast_fusion, f32[1536,1,1120]{0,2,1:T(8,128)} %convolution_bitcast_fusion.1), kind=kLoop, calls=%fused_computation | loop fusion | flops 3440640 | bytes 27525120 | tf_op jit(solution)/shard_map/stack | solution.py:33
  154.2 44.5 %reduce-scatter.4.cloned.1.call-done = f32[72,1536]{1,0:T(8,128)} async-done(((f32[576,1536]{1,0:T(8,128)}), f32[72,1536]{1,0:T(8,128)}) %reduce-scatter.4.cloned.1.call-update) | async-done | bytes 442384 | tf_op jit(solution)/shard_map/reduce_scatter | solution.py:26
  198.7 1.7 convert_element_type.14
  200.4 62.7 %reduce-scatter.8.cloned.1.call-done = f32[1120,384]{1,0:T(8,128)} async-done(((f32[1120,1536]{1,0:T(8,128)}), f32[1120,384]{1,0:T(8,128)}) %reduce-scatter.8.cloned.1.call-update) | async-done | bytes 1720336 | tf_op jit(solution)/shard_map/reduce_scatter | solution.py:38
  263.1 2.9 broadcast_multiply_fusion
  266.0 106.7 %reduce-scatter.6.cloned.1.call-done = f32[384,2,1120]{0,2,1:T(8,128)} async-done(((f32[1536,2,1120]{0,2,1:T(8,128)}), f32[384,2,1120]{0,2,1:T(8,128)}) %reduce-scatter.6.cloned.1.call-update) | async-done | bytes 3440656 | tf_op jit(solution)/shard_map/reduce_scatter | solution.py:32
  372.7 4.0 %fusion.1 = (f32[384,1120]{0,1:T(8,128)}, f32[384,1120]{0,1:T(8,128)}) fusion(f32[384,2,1120]{0,2,1:T(8,128)} %reduce-scatter.6.cloned.1.call-done), kind=kLoop, calls=%fused_computation.10 | loop fusion | flops 860160 | bytes 6881280 | tf_op jit(solution)/shard_map/div | solution.py:42
  (23 shorter events, 0.2 us)
Async XLA Ops:
  7.2 51.7 %copy-start = (bf16[1536,1120]{0,1:T(8,128)(2,1)S(1)}, bf16[1536,1120]{0,1:T(8,128)(2,1)}, u32[]{:S(2)}) copy-start(bf16[1536,1120]{0,1:T(8,128)(2,1)} %param.7) | copy-start | bytes 10321924
  7.2 51.7 %all-gather.5.cloned.1.call-start = ((), (), s32[]{:S(2)}) async-start(), calls=%async_computation.4 | async-start | bytes 1990656 | tf_op jit(solution)/shard_map/all_gather | solution.py:15
  7.9 98.1 %all-gather.3.cloned.1.call-start = ((), (), s32[]{:S(2)}) async-start(), calls=%async_computation.3 | async-start | bytes 1990656 | tf_op jit(solution)/shard_map/all_gather | solution.py:21
  8.7 190.1 %reduce-scatter.4.cloned.1.call-start = ((), (), s32[]{:S(2)}) async-start(), calls=%async_computation.5 | async-start | bytes 3981312 | tf_op jit(solution)/shard_map/reduce_scatter | solution.py:26
  58.9 5.6 %copy-start.2 = (bf16[1536,1120]{0,1:T(8,128)(2,1)S(1)}, bf16[1536,1120]{0,1:T(8,128)(2,1)}, u32[]{:S(2)}) copy-start(bf16[1536,1120]{0,1:T(8,128)(2,1)} %param.8) | copy-start | bytes 10321924
  58.9 5.6 %copy-start.4 = (bf16[576,1536]{1,0:T(8,128)(2,1)S(1)}, bf16[576,1536]{1,0:T(8,128)(2,1)}, u32[]{:S(2)}) copy-start(bf16[576,1536]{1,0:T(8,128)(2,1)} %all-gather.5.cloned.1.call-done) | copy-start | bytes 5308420
  113.1 2.5 copy-start.7
  113.1 2.5 copy-start.9
  113.1 2.9 copy-start.3
  120.4 1.5 copy-start.6
  120.4 142.7 %reduce-scatter.8.cloned.1.call-start = ((), (), s32[]{:S(2)}) async-start(), calls=%async_computation.7 | async-start | bytes 8601600 | tf_op jit(solution)/shard_map/reduce_scatter | solution.py:38
  129.9 1.5 copy-start.5
  130.0 7.8 %copy-start.8 = (bf16[576,1120]{1,0:T(8,128)(2,1)S(1)}, bf16[576,1120]{1,0:T(8,128)(2,1)}, u32[]{:S(2)}) copy-start(bf16[576,1120]{1,0:T(8,128)(2,1)} %copy-done.7) | copy-start | bytes 3870724
  130.0 242.7 %reduce-scatter.6.cloned.1.call-start = ((), (), s32[]{:S(2)}) async-start(), calls=%async_computation.6 | async-start | bytes 17203200 | tf_op jit(solution)/shard_map/reduce_scatter | solution.py:32
  263.1 113.5 %copy-start.1 = (bf16[1536,1120]{0,1:T(8,128)(2,1)S(1)}, bf16[1536,1120]{0,1:T(8,128)(2,1)}, u32[]{:S(2)}) copy-start(bf16[1536,1120]{0,1:T(8,128)(2,1)} %param.7) | copy-start | bytes 10321924
Sparse Core Ops, SparseCore 0:
  10.2 48.6 all-gather.4
  61.0 44.9 all-gather.2
  120.5 78.1 reduce-scatter.3
  201.1 61.9 reduce-scatter.7
  265.7 106.9 reduce-scatter.5
where the time goes:
time: 383 us
  waiting for transfers between devices  303 us (79%)
  matrix products  42.7 us (11%)
  other arithmetic  20.1 us (5%)
  between operations  13.9 us (4%)
    reduce_scatter x1, waiting for transfers between devices, on_device(): lax.psum_scatter(jnp.stack((contract(whole, dgate, 0, 0), contract(whole,...  107 us
    reduce_scatter x1, waiting for transfers between devices, on_device(): lax.psum_scatter(down_part, 'dp', scatter_dimension=1, tiled=True)  62.7 us
    all_gather x1, waiting for transfers between devices, on_device(): whole = lax.all_gather(normed, 'tensor', axis=0, tiled=True)  50.1 us
    reduce_scatter x1, waiting for transfers between devices, on_device(): lax.psum_scatter(contract(dgate, gate_weight, 1, 1) + contract(dup, up_we...  44.5 us
    all_gather x1, waiting for transfers between devices, on_device(): piece = lax.all_gather(out_grad, 'tensor', axis=0, tiled=True)  37.5 us
    dot_general x6, matrix products, contract(): lax.dot_general(left, right, (((left_dim,), (right_dim,)), ((), ())), pre...  33.1 us
    another operation x1, other arithmetic, on_device(): jnp.stack((contract(whole, dgate, 0, 0), contract(whole, dup, 0, 0)), 1)  11.6 us
  transfers between devices with their start and end apart: 5, of which 5 were waited for; matrix products, arithmetic and copies ran while one was open for 12% of the time, Pallas kernels for 0%

commit v1 on v0

--- a/solution.py
+++ b/solution.py
@@ -1,13 +1,349 @@
 import jax
 import jax.numpy as jnp
 from jax import lax
+from jax.experimental import pallas as pl
+from jax.experimental.pallas import tpu as pltpu
 from jax.sharding import PartitionSpec as P
+
+F32, BF16 = jnp.float32, jnp.bfloat16
+MESH = pl.DeviceIdType.MESH
+LINE = 4
 
 
 def contract(left, right, left_dim, right_dim):
     return lax.dot_general(
         left, right, (((left_dim,), (right_dim,)), ((), ())), preferred_element_type=jnp.float32
     )
+
+
+def kernel(
+    normed, out_grad, gate_w, up_w, down_w,
+    grad_in, grad_gate, grad_up, grad_down,
+    blocks, weights, flat, pre, post, acc, dw_send, dw_recv,
+    gi, gi_send, gi_recv, zs, zr, gi_out,
+    local_sem, out_sem, recv_sem, send_sem, relay_sem,
+    dws_sem, dwr_sem, gxs_sem, gxr_sem, gzs_sem, gzr_sem,
+):
+    rows, width = normed.shape
+    hid = gate_w.shape[0]
+    chunk = pre.shape[2]
+    n_chunks = hid // chunk
+    window = 2 * LINE * rows
+    quarter = width // 4
+    dp, tp = lax.axis_index("dp"), lax.axis_index("tensor")
+    y, core = dp // 2, dp % 2
+    z, x = tp // 2, tp % 2
+    across_x = {"tensor": 2 * z + 1 - x}
+    across_y = {"dp": 2 * (1 - y) + core}
+    across_core = {"dp": 2 * y + 1 - core}
+
+    own = [
+        pltpu.make_async_copy(src, blocks.at[a, 0, tp], local_sem.at[a])
+        for a, src in enumerate((normed, out_grad))
+    ]
+    loads = [
+        pltpu.make_async_copy(src, weights.at[i], local_sem.at[2 + i])
+        for i, src in enumerate((gate_w, up_w, down_w))
+    ]
+    for copy in own + loads:
+        copy.start()
+
+    barrier = pltpu.get_barrier_semaphore()
+    for where in (across_x, across_y, across_core):
+        pl.semaphore_signal(barrier, inc=1, device_id=where, device_id_type=MESH)
+    for d in range(1, LINE):
+        pl.semaphore_signal(
+            barrier, inc=1, device_id={"tensor": 2 * ((z + d) % LINE) + x}, device_id_type=MESH
+        )
+    pl.semaphore_wait(barrier, 3 + LINE - 1)
+
+    def move(a, w_from, w_to, block, sem, where):
+        return pltpu.make_async_remote_copy(
+            src_ref=blocks.at[a, w_from, block],
+            dst_ref=blocks.at[a, w_to, block],
+            send_sem=sem,
+            recv_sem=recv_sem.at[a, w_to, block],
+            device_id=where,
+            device_id_type=MESH,
+        )
+
+    def arrived(a, w, block):
+        move(a, w, w, block, send_sem.at[a, 0, 0], across_x).wait_recv()
+
+    def to_sides(a, line):
+        block = 2 * line + x
+        move(a, 0, 0, block, send_sem.at[a, 0, line], across_x).start()
+        move(a, 0, 1, block, send_sem.at[a, 1, line], across_y).start()
+
+    def up_copy(a, line):
+        return move(a, 0, 0, 2 * line + x, send_sem.at[a, 2, line], {"tensor": 2 * (z + 1) + x})
+
+    def down_copy(a, line):
+        return move(a, 0, 0, 2 * line + x, send_sem.at[a, 3, line], {"tensor": 2 * (z - 1) + x})
+
+    def first(a):
+        own[a].wait()
+
+        @pl.when(z < LINE - 1)
+        def _():
+            up_copy(a, z).start()
+
+        @pl.when(z > 0)
+        def _():
+            down_copy(a, z).start()
+
+        to_sides(a, z)
+
+    def step(a, s):
+        @pl.when(z >= s)
+        def _():
+            arrived(a, 0, 2 * (z - s) + x)
+            if s < LINE - 1:
+                @pl.when(z < LINE - 1)
+                def _():
+                    up_copy(a, z - s).start()
+            to_sides(a, z - s)
+
+        @pl.when(z + s < LINE)
+        def _():
+            arrived(a, 0, 2 * (z + s) + x)
+            if s < LINE - 1:
+                @pl.when(z > 0)
+                def _():
+                    down_copy(a, z + s).start()
+            to_sides(a, z + s)
+
+    def in_order(act):
+        act(z)
+        for s in range(1, LINE):
+            pl.when(z >= s)(lambda s=s: act(z - s))
+            pl.when(z + s < LINE)(lambda s=s: act(z + s))
+
+    def flatten(a, w):
+        flat[a] = blocks[a, w].astype(F32).reshape(window, width).astype(BF16)
+
+    def part(j):
+        return pl.ds(pl.multiple_of(j * chunk, 16), chunk)
+
+    def backward(j, gate, up):
+        sig = jax.nn.sigmoid(gate)
+        act = gate * sig
+        dhid = contract(weights[2, part(j), :], flat[1], 1, 1)
+        post[2, j] = (act * up).astype(BF16)
+        post[0, j] = (dhid * up * sig * (1.0 + gate * (1.0 - sig))).astype(BF16)
+        post[1, j] = (dhid * act).astype(BF16)
+
+    def halves(a):
+        mine = flat[a, :, pl.ds(pl.multiple_of(dp * quarter, 128), quarter)]
+        other = flat[a, :, pl.ds(pl.multiple_of((2 * y + 1 - core) * quarter, 128), quarter)]
+        return jnp.concatenate([mine, other], axis=1)
+
+    first(0)
+    step(0, 1)
+    first(1)
+    step(0, 2)
+    step(0, 3)
+    for line in range(LINE):
+        arrived(0, 0, 2 * line + 1 - x)
+    flatten(0, 0)
+    step(1, 1)
+    loads[0].wait()
+    loads[1].wait()
+
+    @pl.loop(0, n_chunks)
+    def _(j):
+        pre[0, j] = contract(weights[0, part(j), :], flat[0], 1, 1)
+        pre[1, j] = contract(weights[1, part(j), :], flat[0], 1, 1)
+
+    step(1, 2)
+    step(1, 3)
+
+    def relay_x(line):
+        arrived(0, 1, 2 * line + x)
+        move(0, 1, 1, 2 * line + x, relay_sem.at[0, line], across_x).start()
+
+    def relay_y(line):
+        arrived(1, 0, 2 * line + 1 - x)
+        move(1, 0, 1, 2 * line + 1 - x, relay_sem.at[1, line], across_y).start()
+
+    in_order(relay_x)
+    in_order(relay_y)
+    flatten(1, 0)
+    loads[2].wait()
+
+    @pl.loop(0, n_chunks)
+    def _(j):
+        backward(j, pre[0, j], pre[1, j])
+
+    half = width // 2
+
+    for n in range(2):
+        cols = slice(n * half, (n + 1) * half)
+        total = contract(post[0].reshape(hid, window), weights[0, :, cols], 0, 0)
+        total += contract(post[1].reshape(hid, window), weights[1, :, cols], 0, 0)
+        gi[:, :, cols] = total.reshape(2 * LINE, rows, half)
+
+    def gi_x(line):
+        return pltpu.make_async_remote_copy(
+            src_ref=gi_send.at[line], dst_ref=gi_recv.at[line],
+            send_sem=gxs_sem.at[line], recv_sem=gxr_sem.at[line],
+            device_id=across_x, device_id_type=MESH,
+        )
+
+    def gi_z(d):
+        return pltpu.make_async_remote_copy(
+            src_ref=zs.at[d - 1], dst_ref=zr.at[d - 1],
+            send_sem=gzs_sem.at[d - 1], recv_sem=gzr_sem.at[d - 1],
+            device_id={"tensor": 2 * ((z + d) % LINE) + x}, device_id_type=MESH,
+        )
+
+    for d in (2, 1, 3, 0):
+        line = (z + d) % LINE
+        gi_send[line] = gi[2 * line + 1 - x].astype(BF16)
+        gi_x(line).start()
+
+    @pl.loop(0, n_chunks)
+    def _(j):
+        for m, a in ((0, 0), (1, 0), (2, 1)):
+            acc[m, part(j), :] = contract(post[m, j], halves(a), 1, 0)
+
+    for d in (2, 1, 3):
+        line = (z + d) % LINE
+        gi_x(line).wait_recv()
+        zs[d - 1] = (gi[2 * line + x] + gi_recv[line].astype(F32)).astype(BF16)
+        gi_z(d).start()
+    gi_x(z).wait_recv()
+
+    for line in range(LINE):
+        arrived(0, 1, 2 * line + 1 - x)
+    flatten(0, 1)
+    for line in range(LINE):
+        arrived(1, 1, 2 * line + x)
+        arrived(1, 1, 2 * line + 1 - x)
+    flatten(1, 1)
+
+    def dw_copy(m, j):
+        return pltpu.make_async_remote_copy(
+            src_ref=dw_send.at[m, j], dst_ref=dw_recv.at[m, j],
+            send_sem=dws_sem.at[m, j], recv_sem=dwr_sem.at[m, j],
+            device_id=across_core, device_id_type=MESH,
+        )
+
+    @pl.loop(0, n_chunks)
+    def _(j):
+        gate = contract(weights[0, part(j), :], flat[0], 1, 1)
+        up = contract(weights[1, part(j), :], flat[0], 1, 1)
+        backward(j, gate, up)
+        for m, a in ((0, 0), (1, 0), (2, 1)):
+            total = acc[m, part(j), :] + contract(post[m, j], halves(a), 1, 0)
+            acc[m, part(j), :] = total
+            dw_send[m, j] = total[:, quarter:].astype(BF16)
+            dw_copy(m, j).start()
+
+    total = gi[tp] + gi_recv[z].astype(F32)
+    for d in range(1, LINE):
+        gi_z(d).wait_recv()
+        total += zr[d - 1].astype(F32)
+    gi_out[...] = total.astype(BF16)
+    gi_done = pltpu.make_async_copy(gi_out, grad_in, local_sem.at[0])
+    gi_done.start()
+
+    outs = (grad_gate, grad_up, grad_down)
+
+    def write(m, j):
+        return pltpu.make_async_copy(
+            acc.at[m, part(j), pl.ds(0, quarter)], outs[m].at[part(j), :], out_sem.at[m, j]
+        )
+
+    @pl.loop(0, n_chunks)
+    def _(j):
+        for m in range(3):
+            dw_copy(m, j).wait_recv()
+            acc[m, part(j), pl.ds(0, quarter)] += dw_recv[m, j].astype(F32)
+            write(m, j).start()
+
+    gi_done.wait()
+
+    @pl.loop(0, n_chunks)
+    def _(j):
+        for m in range(3):
+            dw_copy(m, j).wait_send()
+            write(m, j).wait()
+
+    for line in range(LINE):
+        gi_x(line).wait_send()
+        move(0, 1, 1, 2 * line + x, relay_sem.at[0, line], across_x).wait_send()
+        move(1, 0, 1, 2 * line + 1 - x, relay_sem.at[1, line], across_y).wait_send()
+        for a in range(2):
+            move(a, 0, 0, 2 * line + x, send_sem.at[a, 0, line], across_x).wait_send()
+            move(a, 0, 1, 2 * line + x, send_sem.at[a, 1, line], across_y).wait_send()
+
+            @pl.when((z < LINE - 1) & (line <= z))
+            def _():
+                up_copy(a, line).wait_send()
+
+            @pl.when((z > 0) & (line >= z))
+            def _():
+                down_copy(a, line).wait_send()
+    for d in range(1, LINE):
+        gi_z(d).wait_send()
+
+
+def fused(normed, out_grad, gate_weight, up_weight, down_weight):
+    rows, width = normed.shape
+    hid = down_weight.shape[0]
+    chunks = 5
+    chunk = hid // chunks
+    window = 2 * LINE * rows
+    quarter = width // 4
+    dma = pltpu.SemaphoreType.DMA
+    anywhere = pl.BlockSpec(memory_space=pl.ANY)
+    outs = pl.pallas_call(
+        kernel,
+        out_shape=(
+            jax.ShapeDtypeStruct((rows, width), BF16),
+            jax.ShapeDtypeStruct((hid, quarter), F32),
+            jax.ShapeDtypeStruct((hid, quarter), F32),
+            jax.ShapeDtypeStruct((hid, quarter), F32),
+        ),
+        in_specs=[anywhere] * 5,
+        out_specs=(anywhere,) * 4,
+        scratch_shapes=[
+            pltpu.VMEM((2, 2, 2 * LINE, rows, width), BF16),
+            pltpu.VMEM((3, hid, width), BF16),
+            pltpu.VMEM((2, window, width), BF16),
+            pltpu.VMEM((2, chunks, chunk, window), F32),
+            pltpu.VMEM((3, chunks, chunk, window), BF16),
+            pltpu.VMEM((3, hid, width // 2), F32),
+            pltpu.VMEM((3, chunks, chunk, quarter), BF16),
+            pltpu.VMEM((3, chunks, chunk, quarter), BF16),
+            pltpu.VMEM((2 * LINE, rows, width), F32),
+            pltpu.VMEM((LINE, rows, width), BF16),
+            pltpu.VMEM((LINE, rows, width), BF16),
+            pltpu.VMEM((LINE - 1, rows, width), BF16),
+            pltpu.VMEM((LINE - 1, rows, width), BF16),
+            pltpu.VMEM((rows, width), BF16),
+            dma((5,)),
+            dma((3, chunks)),
+            dma((2, 2, 2 * LINE)),
+            dma((2, 4, LINE)),
+            dma((2, LINE)),
+            dma((3, chunks)),
+            dma((3, chunks)),
+            dma((LINE,)),
+            dma((LINE,)),
+            dma((LINE - 1,)),
+            dma((LINE - 1,)),
+        ],
+        compiler_params=pltpu.CompilerParams(
+            collective_id=0, has_side_effects=True, vmem_limit_bytes=63 * 2**20
+        ),
+        cost_estimate=pl.CostEstimate(
+            flops=22 * window * width * hid, bytes_accessed=6 * width * hid, transcendentals=0
+        ),
+    )(normed, out_grad, gate_weight.T, up_weight.T, down_weight)
+    replicas = lax.axis_size("dp")
+    return outs[0], outs[1].T / replicas, outs[2].T / replicas, outs[3] / replicas
 
 
 def on_device(normed, out_grad, gate_weight, up_weight, down_weight):
@@ -45,8 +381,9 @@
 
 
 def solution(mesh):
+    small = mesh.shape["dp"] == 4 and mesh.shape["tensor"] == 2 * LINE
     return jax.shard_map(
-        on_device,
+        fused if small else on_device,
         mesh=mesh,
         in_specs=(
             P(("dp", "tensor"), None),

time: 383 us -> 114 us (0.30)
  waiting for transfers between devices: 303 us -> 0 us
  Pallas kernels: 0 us -> 108 us
  matrix products: 42.7 us -> 0 us
  other arithmetic: 20.1 us -> 4.89 us
  between operations: 13.9 us -> 0.66 us
    reduce_scatter x3 -> x0, waiting for transfers between devices: 214 us -> none  [the longest x1 107 us: on_device(): lax.psum_scatter(jnp.stack((contract(whole, dgate, 0, 0), contract(whole,...]
    pallas_call x0 -> x1, Pallas kernels: none -> 108 us  [fused(): pl.pallas_call(kernel, out_shape=(jax.ShapeDtypeStruct((rows, width), BF1...]
    all_gather x2 -> x0, waiting for transfers between devices: 87.6 us -> none  [the longest x1 50.1 us: on_device(): whole = lax.all_gather(normed, 'tensor', axis=0, tiled=True)]
    dot_general x8 -> x0, matrix products: 42.7 us -> none  [the longest x6 33.1 us: contract(): lax.dot_general(left, right, (((left_dim,), (right_dim,)), ((), ())), pre...]
    another operation x1 -> x0, other arithmetic: 11.6 us -> none  [on_device(): jnp.stack((contract(whole, dgate, 0, 0), contract(whole, dup, 0, 0)), 1)]
  transfers between devices with their start and end apart: 5 -> 0, of which waited for: 5 -> 0; matrix products, arithmetic and copies ran while one was open for 12% -> 0% of each run, Pallas kernels for 0% -> 0%
where the time goes in v1:
time: 114 us
  Pallas kernels  108 us (95%)
  other arithmetic  4.89 us (4%)
    pallas_call x1, Pallas kernels, fused(): pl.pallas_call(kernel, out_shape=(jax.ShapeDtypeStruct((rows, width), BF1...  108 us
    div x1, other arithmetic, fused(): outs[3] / replicas  2.91 us

profile of v1, /device:TPU:0, one launch (start us, length us, event | category | flops | bytes accessed | tf_op | source)
XLA Modules:
  0.0 113.9 jit_solution(13274399373420071996)
XLA Ops:
  0.6 107.7 %shard_map.84 = (bf16[72,1536]{1,0:T(8,128)(2,1)}, f32[1120,384]{1,0:T(8,128)}, f32[1120,384]{1,0:T(8,128)}, f32[1120,384]{1,0:T(8,128)}) custom-call(bf16[72,1536]{1,0:T(8,128)(2,1)} %normed.1, bf16[72,1536]{1,0:T(8,128)(2,1)} %out_grad.1, bf16[1120,1536]{1,0:T(8,128)(2,1)} %bitcast.6, bf16[1120,1536]{1,0:T(8,128)(2,1)} %bitcast.7, bf16[1120,1536]{1,0:T(8,128)(2,1)} %down_w.1), custom_call_target="tpu_custom_call" | custom-call | flops 21799895040 | bytes 10321920 | tf_op jit(solution)/shard_map/pallas_call | solution.py:301
  108.3 0.0 copy-start
  108.3 0.0 copy-start.1
  108.3 2.9 %broadcast_multiply_fusion = f32[1120,384]{1,0:T(8,128)} fusion(f32[1120,384]{1,0:T(8,128)} %get-tuple-element.11), kind=kLoop, calls=%fused_computation.2 | loop fusion | flops 430080 | bytes 3440640 | tf_op jit(solution)/shard_map/div | solution.py:346
  111.2 0.0 copy-done
  111.2 0.0 copy-done.1
  111.2 0.0 copy-start.2
  111.2 2.0 %multiply_bitcast_fusion = (f32[384,1120]{0,1:T(8,128)}, f32[384,1120]{0,1:T(8,128)}) fusion(f32[1120,384]{1,0:T(8,128)S(1)} %copy-done.1, f32[1120,384]{1,0:T(8,128)S(1)} %copy-done), kind=kLoop, calls=%fused_computation | loop fusion | flops 860160 | bytes 6881280 | tf_op jit(solution)/shard_map/div | solution.py:346
  113.2 0.0 copy-done.2
  113.2 0.7 copy.10
Async XLA Ops:
  108.3 2.9 %copy-start = (f32[1120,384]{1,0:T(8,128)S(1)}, f32[1120,384]{1,0:T(8,128)}, u32[]{:S(2)}) copy-start(f32[1120,384]{1,0:T(8,128)} %get-tuple-element.9) | copy-start | bytes 5160964
  108.3 2.9 %copy-start.1 = (f32[1120,384]{1,0:T(8,128)S(1)}, f32[1120,384]{1,0:T(8,128)}, u32[]{:S(2)}) copy-start(f32[1120,384]{1,0:T(8,128)} %get-tuple-element.10) | copy-start | bytes 5160964
  111.2 2.0 %copy-start.2 = (bf16[72,1536]{1,0:T(8,128)(2,1)S(1)}, bf16[72,1536]{1,0:T(8,128)(2,1)}, u32[]{:S(2)}) copy-start(bf16[72,1536]{1,0:T(8,128)(2,1)} %get-tuple-element.18) | copy-start | bytes 663556

commit v2 on v1

--- a/solution.py
+++ b/solution.py
@@ -19,7 +19,7 @@
 def kernel(
     normed, out_grad, gate_w, up_w, down_w,
     grad_in, grad_gate, grad_up, grad_down,
-    blocks, weights, flat, pre, post, acc, dw_send, dw_recv,
+    blocks, weights, flat, half, turned, pre, post, acc, dw_send, dw_recv,
     gi, gi_send, gi_recv, zs, zr, gi_out,
     local_sem, out_sem, recv_sem, send_sem, relay_sem,
     dws_sem, dwr_sem, gxs_sem, gxr_sem, gzs_sem, gzr_sem,
@@ -119,8 +119,15 @@
             pl.when(z >= s)(lambda s=s: act(z - s))
             pl.when(z + s < LINE)(lambda s=s: act(z + s))
 
-    def flatten(a, w):
-        flat[a] = blocks[a, w].astype(F32).reshape(window, width).astype(BF16)
+    def flatten(a, w, line):
+        pair = blocks[a, w, pl.ds(2 * line, 2)].astype(F32).reshape(2 * rows, width)
+        flat[a, pl.ds(pl.multiple_of(2 * rows * line, 16), 2 * rows), :] = pair.astype(BF16)
+
+    def share(a):
+        mine = pl.ds(pl.multiple_of(dp * quarter, 128), quarter)
+        other = pl.ds(pl.multiple_of((2 * y + 1 - core) * quarter, 128), quarter)
+        half[a, :, :quarter] = flat[a, :, mine]
+        half[a, :, quarter:] = flat[a, :, other]
 
     def part(j):
         return pl.ds(pl.multiple_of(j * chunk, 16), chunk)
@@ -133,11 +140,6 @@
         post[0, j] = (dhid * up * sig * (1.0 + gate * (1.0 - sig))).astype(BF16)
         post[1, j] = (dhid * act).astype(BF16)
 
-    def halves(a):
-        mine = flat[a, :, pl.ds(pl.multiple_of(dp * quarter, 128), quarter)]
-        other = flat[a, :, pl.ds(pl.multiple_of((2 * y + 1 - core) * quarter, 128), quarter)]
-        return jnp.concatenate([mine, other], axis=1)
-
     first(0)
     step(0, 1)
     first(1)
@@ -145,7 +147,7 @@
     step(0, 3)
     for line in range(LINE):
         arrived(0, 0, 2 * line + 1 - x)
-    flatten(0, 0)
+        flatten(0, 0, line)
     step(1, 1)
     loads[0].wait()
     loads[1].wait()
@@ -165,23 +167,25 @@
     def relay_y(line):
         arrived(1, 0, 2 * line + 1 - x)
         move(1, 0, 1, 2 * line + 1 - x, relay_sem.at[1, line], across_y).start()
+        flatten(1, 0, line)
 
     in_order(relay_x)
+    share(0)
     in_order(relay_y)
-    flatten(1, 0)
     loads[2].wait()
 
     @pl.loop(0, n_chunks)
     def _(j):
         backward(j, pre[0, j], pre[1, j])
 
-    half = width // 2
-
+    for m in range(2):
+        turned[m] = post[m].reshape(hid, window).T
+    share(1)
     for n in range(2):
-        cols = slice(n * half, (n + 1) * half)
-        total = contract(post[0].reshape(hid, window), weights[0, :, cols], 0, 0)
-        total += contract(post[1].reshape(hid, window), weights[1, :, cols], 0, 0)
-        gi[:, :, cols] = total.reshape(2 * LINE, rows, half)
+        cols = slice(n * 2 * quarter, (n + 1) * 2 * quarter)
+        total = contract(turned[0], weights[0, :, cols], 1, 0)
+        total += contract(turned[1], weights[1, :, cols], 1, 0)
+        gi[:, :, cols] = total.reshape(2 * LINE, rows, 2 * quarter)
 
     def gi_x(line):
         return pltpu.make_async_remote_copy(
@@ -205,7 +209,7 @@
     @pl.loop(0, n_chunks)
     def _(j):
         for m, a in ((0, 0), (1, 0), (2, 1)):
-            acc[m, part(j), :] = contract(post[m, j], halves(a), 1, 0)
+            acc[m, part(j), :] = contract(post[m, j], half[a], 1, 0)
 
     for d in (2, 1, 3):
         line = (z + d) % LINE
@@ -216,11 +220,13 @@
 
     for line in range(LINE):
         arrived(0, 1, 2 * line + 1 - x)
-    flatten(0, 1)
+        flatten(0, 1, line)
+    share(0)
     for line in range(LINE):
         arrived(1, 1, 2 * line + x)
         arrived(1, 1, 2 * line + 1 - x)
-    flatten(1, 1)
+        flatten(1, 1, line)
+    share(1)
 
     def dw_copy(m, j):
         return pltpu.make_async_remote_copy(
@@ -235,7 +241,7 @@
         up = contract(weights[1, part(j), :], flat[0], 1, 1)
         backward(j, gate, up)
         for m, a in ((0, 0), (1, 0), (2, 1)):
-            total = acc[m, part(j), :] + contract(post[m, j], halves(a), 1, 0)
+            total = acc[m, part(j), :] + contract(post[m, j], half[a], 1, 0)
             acc[m, part(j), :] = total
             dw_send[m, j] = total[:, quarter:].astype(BF16)
             dw_copy(m, j).start()
@@ -292,7 +298,7 @@
 def fused(normed, out_grad, gate_weight, up_weight, down_weight):
     rows, width = normed.shape
     hid = down_weight.shape[0]
-    chunks = 5
+    chunks = 2
     chunk = hid // chunks
     window = 2 * LINE * rows
     quarter = width // 4
@@ -312,6 +318,8 @@
             pltpu.VMEM((2, 2, 2 * LINE, rows, width), BF16),
             pltpu.VMEM((3, hid, width), BF16),
             pltpu.VMEM((2, window, width), BF16),
+            pltpu.VMEM((2, window, width // 2), BF16),
+            pltpu.VMEM((2, window, hid), BF16),
             pltpu.VMEM((2, chunks, chunk, window), F32),
             pltpu.VMEM((3, chunks, chunk, window), BF16),
             pltpu.VMEM((3, hid, width // 2), F32),

time: 114 us -> 110 us (0.965)
  Pallas kernels: 108 us -> 103 us
    pallas_call x1, Pallas kernels: 108 us -> 103 us  [fused(): pl.pallas_call(kernel, out_shape=(jax.ShapeDtypeStruct((rows, width), BF1...]
where the time goes in v2:
time: 110 us
  Pallas kernels  103 us (94%)
  other arithmetic  4.89 us (4%)
    pallas_call x1, Pallas kernels, fused(): pl.pallas_call(kernel, out_shape=(jax.ShapeDtypeStruct((rows, width), BF1...  103 us
    div x1, other arithmetic, fused(): outs[3] / replicas  2.91 us

profile of v2, /device:TPU:0, one launch (start us, length us, event | category | flops | bytes accessed | tf_op | source)
XLA Modules:
  0.0 109.6 jit_solution(5111544317064098707)
XLA Ops:
  0.6 103.3 %shard_map.84 = (bf16[72,1536]{1,0:T(8,128)(2,1)}, f32[1120,384]{1,0:T(8,128)}, f32[1120,384]{1,0:T(8,128)}, f32[1120,384]{1,0:T(8,128)}) custom-call(bf16[72,1536]{1,0:T(8,128)(2,1)} %normed.1, bf16[72,1536]{1,0:T(8,128)(2,1)} %out_grad.1, bf16[1120,1536]{1,0:T(8,128)(2,1)} %bitcast.6, bf16[1120,1536]{1,0:T(8,128)(2,1)} %bitcast.7, bf16[1120,1536]{1,0:T(8,128)(2,1)} %down_w.1), custom_call_target="tpu_custom_call" | custom-call | flops 21799895040 | bytes 10321920 | tf_op jit(solution)/shard_map/pallas_call | solution.py:307
  104.0 0.0 copy-start
  104.0 0.0 copy-start.1
  104.0 2.9 %broadcast_multiply_fusion = f32[1120,384]{1,0:T(8,128)} fusion(f32[1120,384]{1,0:T(8,128)} %get-tuple-element.11), kind=kLoop, calls=%fused_computation.2 | loop fusion | flops 430080 | bytes 3440640 | tf_op jit(solution)/shard_map/div | solution.py:354
  106.9 0.0 copy-done
  106.9 0.0 copy-done.1
  106.9 0.0 copy-start.2
  106.9 2.0 %multiply_bitcast_fusion = (f32[384,1120]{0,1:T(8,128)}, f32[384,1120]{0,1:T(8,128)}) fusion(f32[1120,384]{1,0:T(8,128)S(1)} %copy-done.1, f32[1120,384]{1,0:T(8,128)S(1)} %copy-done), kind=kLoop, calls=%fused_computation | loop fusion | flops 860160 | bytes 6881280 | tf_op jit(solution)/shard_map/div | solution.py:354
  108.9 0.0 copy-done.2
  108.9 0.7 copy.10
Async XLA Ops:
  104.0 2.9 %copy-start = (f32[1120,384]{1,0:T(8,128)S(1)}, f32[1120,384]{1,0:T(8,128)}, u32[]{:S(2)}) copy-start(f32[1120,384]{1,0:T(8,128)} %get-tuple-element.9) | copy-start | bytes 5160964
  104.0 2.9 %copy-start.1 = (f32[1120,384]{1,0:T(8,128)S(1)}, f32[1120,384]{1,0:T(8,128)}, u32[]{:S(2)}) copy-start(f32[1120,384]{1,0:T(8,128)} %get-tuple-element.10) | copy-start | bytes 5160964
  106.9 2.0 %copy-start.2 = (bf16[72,1536]{1,0:T(8,128)(2,1)S(1)}, bf16[72,1536]{1,0:T(8,128)(2,1)}, u32[]{:S(2)}) copy-start(bf16[72,1536]{1,0:T(8,128)(2,1)} %get-tuple-element.18) | copy-start | bytes 663556

commit v3 on v2

--- a/solution.py
+++ b/solution.py
@@ -19,7 +19,7 @@
 def kernel(
     normed, out_grad, gate_w, up_w, down_w,
     grad_in, grad_gate, grad_up, grad_down,
-    blocks, weights, flat, half, turned, pre, post, acc, dw_send, dw_recv,
+    blocks, weights, flat, half, turned, pre, post, dhid, acc, dw_recv,
     gi, gi_send, gi_recv, zs, zr, gi_out,
     local_sem, out_sem, recv_sem, send_sem, relay_sem,
     dws_sem, dwr_sem, gxs_sem, gxr_sem, gzs_sem, gzr_sem,
@@ -75,43 +75,47 @@
         move(a, 0, 0, block, send_sem.at[a, 0, line], across_x).start()
         move(a, 0, 1, block, send_sem.at[a, 1, line], across_y).start()
 
-    def up_copy(a, line):
-        return move(a, 0, 0, 2 * line + x, send_sem.at[a, 2, line], {"tensor": 2 * (z + 1) + x})
-
-    def down_copy(a, line):
-        return move(a, 0, 0, 2 * line + x, send_sem.at[a, 3, line], {"tensor": 2 * (z - 1) + x})
-
-    def first(a):
-        own[a].wait()
-
+    def chain(c, line, way):
+        a, w, column = ((0, 0, x), (1, 0, x), (0, 1, 1 - x))[c]
+        sem = send_sem.at[c, 2 if way > 0 else 3, line]
+        return move(a, w, w, 2 * line + column, sem, {"tensor": 2 * (z + way) + x})
+
+    def landed(c, line):
+        a, w, column = ((0, 0, x), (1, 0, x), (0, 1, 1 - x))[c]
+        arrived(a, w, 2 * line + column)
+
+    def first(c):
         @pl.when(z < LINE - 1)
         def _():
-            up_copy(a, z).start()
+            chain(c, z, 1).start()
 
         @pl.when(z > 0)
         def _():
-            down_copy(a, z).start()
-
-        to_sides(a, z)
-
-    def step(a, s):
+            chain(c, z, -1).start()
+
+        if c < 2:
+            to_sides(c, z)
+
+    def step(c, s):
         @pl.when(z >= s)
         def _():
-            arrived(a, 0, 2 * (z - s) + x)
+            landed(c, z - s)
             if s < LINE - 1:
                 @pl.when(z < LINE - 1)
                 def _():
-                    up_copy(a, z - s).start()
-            to_sides(a, z - s)
+                    chain(c, z - s, 1).start()
+            if c < 2:
+                to_sides(c, z - s)
 
         @pl.when(z + s < LINE)
         def _():
-            arrived(a, 0, 2 * (z + s) + x)
+            landed(c, z + s)
             if s < LINE - 1:
                 @pl.when(z > 0)
                 def _():
-                    down_copy(a, z + s).start()
-            to_sides(a, z + s)
+                    chain(c, z + s, -1).start()
+            if c < 2:
+                to_sides(c, z + s)
 
     def in_order(act):
         act(z)
@@ -132,55 +136,80 @@
     def part(j):
         return pl.ds(pl.multiple_of(j * chunk, 16), chunk)
 
-    def backward(j, gate, up):
-        sig = jax.nn.sigmoid(gate)
-        act = gate * sig
-        dhid = contract(weights[2, part(j), :], flat[1], 1, 1)
-        post[2, j] = (act * up).astype(BF16)
-        post[0, j] = (dhid * up * sig * (1.0 + gate * (1.0 - sig))).astype(BF16)
-        post[1, j] = (dhid * act).astype(BF16)
-
+    def forward(j):
+        for m in range(2):
+            pre[m, j] = contract(weights[m, part(j), :], flat[0], 1, 1)
+
+    def backward(j):
+        dhid[...] = contract(weights[2, part(j), :], flat[1], 1, 1)
+
+        def strip(i, _):
+            at = pl.ds(pl.multiple_of(i * 16, 16), 16)
+            gate, up, part_hid = pre[0, j, at, :], pre[1, j, at, :], dhid[at, :]
+            sig = jax.nn.sigmoid(gate)
+            act = gate * sig
+            post[2, j, at, :] = (act * up).astype(BF16)
+            post[0, j, at, :] = (part_hid * up * sig * (1.0 + gate * (1.0 - sig))).astype(BF16)
+            post[1, j, at, :] = (part_hid * act).astype(BF16)
+            return 0
+
+        lax.fori_loop(0, chunk // 16, strip, 0, unroll=5)
+
+    own[0].wait()
     first(0)
     step(0, 1)
+    arrived(0, 1, 2 * z + x)
+    relay_x = move(0, 1, 1, 2 * z + x, relay_sem.at[0, z], across_x)
+    relay_x.start()
+    own[1].wait()
     first(1)
     step(0, 2)
+    arrived(0, 1, 2 * z + 1 - x)
+    first(2)
     step(0, 3)
+    step(1, 1)
+    step(2, 1)
     for line in range(LINE):
         arrived(0, 0, 2 * line + 1 - x)
         flatten(0, 0, line)
-    step(1, 1)
     loads[0].wait()
     loads[1].wait()
+    forward(0)
+    step(1, 2)
+    step(2, 2)
+    forward(1)
+    step(1, 3)
+    step(2, 3)
+
+    far = (z + 2) % LINE
+
+    def relay_y(line):
+        return move(1, 0, 1, 2 * line + 1 - x, relay_sem.at[1, line], across_y)
+
+    relay_far = move(1, 1, 1, 2 * far + x, relay_sem.at[0, far], across_x)
+
+    def relay(line):
+        arrived(1, 0, 2 * line + 1 - x)
+
+        @pl.when(line != far)
+        def _():
+            relay_y(line).start()
+
+        flatten(1, 0, line)
+
+    in_order(relay)
+    arrived(1, 1, 2 * far + x)
+    relay_far.start()
+    share(0)
+    share(1)
+    loads[2].wait()
 
     @pl.loop(0, n_chunks)
     def _(j):
-        pre[0, j] = contract(weights[0, part(j), :], flat[0], 1, 1)
-        pre[1, j] = contract(weights[1, part(j), :], flat[0], 1, 1)
-
-    step(1, 2)
-    step(1, 3)
-
-    def relay_x(line):
-        arrived(0, 1, 2 * line + x)
-        move(0, 1, 1, 2 * line + x, relay_sem.at[0, line], across_x).start()
-
-    def relay_y(line):
-        arrived(1, 0, 2 * line + 1 - x)
-        move(1, 0, 1, 2 * line + 1 - x, relay_sem.at[1, line], across_y).start()
-        flatten(1, 0, line)
-
-    in_order(relay_x)
-    share(0)
-    in_order(relay_y)
-    loads[2].wait()
-
-    @pl.loop(0, n_chunks)
-    def _(j):
-        backward(j, pre[0, j], pre[1, j])
+        backward(j)
 
     for m in range(2):
         turned[m] = post[m].reshape(hid, window).T
-    share(1)
     for n in range(2):
         cols = slice(n * 2 * quarter, (n + 1) * 2 * quarter)
         total = contract(turned[0], weights[0, :, cols], 1, 0)
@@ -219,31 +248,36 @@
     gi_x(z).wait_recv()
 
     for line in range(LINE):
-        arrived(0, 1, 2 * line + 1 - x)
+        @pl.when(line != z)
+        def _():
+            arrived(0, 1, 2 * line + x)
+
         flatten(0, 1, line)
     share(0)
+    pl.loop(0, n_chunks)(forward)
     for line in range(LINE):
-        arrived(1, 1, 2 * line + x)
+        @pl.when(line != far)
+        def _():
+            arrived(1, 1, 2 * line + x)
+
         arrived(1, 1, 2 * line + 1 - x)
         flatten(1, 1, line)
     share(1)
 
     def dw_copy(m, j):
         return pltpu.make_async_remote_copy(
-            src_ref=dw_send.at[m, j], dst_ref=dw_recv.at[m, j],
+            src_ref=post.at[m, j, :, pl.ds(0, quarter)], dst_ref=dw_recv.at[m, j],
             send_sem=dws_sem.at[m, j], recv_sem=dwr_sem.at[m, j],
             device_id=across_core, device_id_type=MESH,
         )
 
     @pl.loop(0, n_chunks)
     def _(j):
-        gate = contract(weights[0, part(j), :], flat[0], 1, 1)
-        up = contract(weights[1, part(j), :], flat[0], 1, 1)
-        backward(j, gate, up)
+        backward(j)
         for m, a in ((0, 0), (1, 0), (2, 1)):
             total = acc[m, part(j), :] + contract(post[m, j], half[a], 1, 0)
             acc[m, part(j), :] = total
-            dw_send[m, j] = total[:, quarter:].astype(BF16)
+            post[m, j, :, :quarter] = total[:, quarter:].astype(BF16)
             dw_copy(m, j).start()
 
     total = gi[tp] + gi_recv[z].astype(F32)
@@ -278,19 +312,25 @@
 
     for line in range(LINE):
         gi_x(line).wait_send()
-        move(0, 1, 1, 2 * line + x, relay_sem.at[0, line], across_x).wait_send()
-        move(1, 0, 1, 2 * line + 1 - x, relay_sem.at[1, line], across_y).wait_send()
+
+        @pl.when(line != far)
+        def _():
+            relay_y(line).wait_send()
+
         for a in range(2):
             move(a, 0, 0, 2 * line + x, send_sem.at[a, 0, line], across_x).wait_send()
             move(a, 0, 1, 2 * line + x, send_sem.at[a, 1, line], across_y).wait_send()
 
+        for c in range(3):
             @pl.when((z < LINE - 1) & (line <= z))
             def _():
-                up_copy(a, line).wait_send()
+                chain(c, line, 1).wait_send()
 
             @pl.when((z > 0) & (line >= z))
             def _():
-                down_copy(a, line).wait_send()
+                chain(c, line, -1).wait_send()
+    relay_x.wait_send()
+    relay_far.wait_send()
     for d in range(1, LINE):
         gi_z(d).wait_send()
 
@@ -322,8 +362,8 @@
             pltpu.VMEM((2, window, hid), BF16),
             pltpu.VMEM((2, chunks, chunk, window), F32),
             pltpu.VMEM((3, chunks, chunk, window), BF16),
+            pltpu.VMEM((chunk, window), F32),
             pltpu.VMEM((3, hid, width // 2), F32),
-            pltpu.VMEM((3, chunks, chunk, quarter), BF16),
             pltpu.VMEM((3, chunks, chunk, quarter), BF16),
             pltpu.VMEM((2 * LINE, rows, width), F32),
             pltpu.VMEM((LINE, rows, width), BF16),
@@ -334,7 +374,7 @@
             dma((5,)),
             dma((3, chunks)),
             dma((2, 2, 2 * LINE)),
-            dma((2, 4, LINE)),
+            dma((3, 4, LINE)),
             dma((2, LINE)),
             dma((3, chunks)),
             dma((3, chunks)),

time: 110 us -> 107 us (0.973)
  Pallas kernels: 103 us -> 101 us
    pallas_call x1, Pallas kernels: 103 us -> 101 us  [fused(): pl.pallas_call(kernel, out_shape=(jax.ShapeDtypeStruct((rows, width), BF1...]
where the time goes in v3:
time: 107 us
  Pallas kernels  101 us (94%)
  other arithmetic  4.89 us (5%)
    pallas_call x1, Pallas kernels, fused(): pl.pallas_call(kernel, out_shape=(jax.ShapeDtypeStruct((rows, width), BF1...  101 us
    div x1, other arithmetic, fused(): outs[3] / replicas  2.91 us

profile of v3, /device:TPU:0, one launch (start us, length us, event | category | flops | bytes accessed | tf_op | source)
XLA Modules:
  0.0 107.0 jit_solution(18241686796463626767)
XLA Ops:
  0.6 100.8 %shard_map.84 = (bf16[72,1536]{1,0:T(8,128)(2,1)}, f32[1120,384]{1,0:T(8,128)}, f32[1120,384]{1,0:T(8,128)}, f32[1120,384]{1,0:T(8,128)}) custom-call(bf16[72,1536]{1,0:T(8,128)(2,1)} %normed.1, bf16[72,1536]{1,0:T(8,128)(2,1)} %out_grad.1, bf16[1120,1536]{1,0:T(8,128)(2,1)} %bitcast.6, bf16[1120,1536]{1,0:T(8,128)(2,1)} %bitcast.7, bf16[1120,1536]{1,0:T(8,128)(2,1)} %down_w.1), custom_call_target="tpu_custom_call" | custom-call | flops 21799895040 | bytes 10321920 | tf_op jit(solution)/shard_map/pallas_call | solution.py:347
  101.4 0.0 copy-start
  101.4 0.0 copy-start.1
  101.5 2.9 %broadcast_multiply_fusion = f32[1120,384]{1,0:T(8,128)} fusion(f32[1120,384]{1,0:T(8,128)} %get-tuple-element.11), kind=kLoop, calls=%fused_computation.2 | loop fusion | flops 430080 | bytes 3440640 | tf_op jit(solution)/shard_map/div | solution.py:394
  104.4 0.0 copy-done
  104.4 0.0 copy-done.1
  104.4 0.0 copy-start.2
  104.4 2.0 %multiply_bitcast_fusion = (f32[384,1120]{0,1:T(8,128)}, f32[384,1120]{0,1:T(8,128)}) fusion(f32[1120,384]{1,0:T(8,128)S(1)} %copy-done.1, f32[1120,384]{1,0:T(8,128)S(1)} %copy-done), kind=kLoop, calls=%fused_computation | loop fusion | flops 860160 | bytes 6881280 | tf_op jit(solution)/shard_map/div | solution.py:394
  106.4 0.0 copy-done.2
  106.4 0.7 copy.10
Async XLA Ops:
  101.4 2.9 %copy-start = (f32[1120,384]{1,0:T(8,128)S(1)}, f32[1120,384]{1,0:T(8,128)}, u32[]{:S(2)}) copy-start(f32[1120,384]{1,0:T(8,128)} %get-tuple-element.9) | copy-start | bytes 5160964
  101.4 2.9 %copy-start.1 = (f32[1120,384]{1,0:T(8,128)S(1)}, f32[1120,384]{1,0:T(8,128)}, u32[]{:S(2)}) copy-start(f32[1120,384]{1,0:T(8,128)} %get-tuple-element.10) | copy-start | bytes 5160964
  104.4 2.0 %copy-start.2 = (bf16[72,1536]{1,0:T(8,128)(2,1)S(1)}, bf16[72,1536]{1,0:T(8,128)(2,1)}, u32[]{:S(2)}) copy-start(bf16[72,1536]{1,0:T(8,128)(2,1)} %get-tuple-element.18) | copy-start | bytes 663556

commit v4 on v3

--- a/solution.py
+++ b/solution.py
@@ -19,17 +19,18 @@
 def kernel(
     normed, out_grad, gate_w, up_w, down_w,
     grad_in, grad_gate, grad_up, grad_down,
-    blocks, weights, flat, half, turned, pre, post, dhid, acc, dw_recv,
+    blocks, weights, flat, half, turned, pre, post, acc, dw_recv,
     gi, gi_send, gi_recv, zs, zr, gi_out,
     local_sem, out_sem, recv_sem, send_sem, relay_sem,
     dws_sem, dwr_sem, gxs_sem, gxr_sem, gzs_sem, gzr_sem,
 ):
     rows, width = normed.shape
     hid = gate_w.shape[0]
-    chunk = pre.shape[2]
+    chunk = pre.shape[3]
     n_chunks = hid // chunk
     window = 2 * LINE * rows
     quarter = width // 4
+    second = half.shape[1] - window
     dp, tp = lax.axis_index("dp"), lax.axis_index("tensor")
     y, core = dp // 2, dp % 2
     z, x = tp // 2, tp % 2
@@ -48,6 +49,10 @@
     for copy in own + loads:
         copy.start()
 
+    gap = slice(second - 128, second)
+    post[:, :, :, gap] = jnp.zeros((3, n_chunks, chunk, 128), BF16)
+    half[:, gap, :] = jnp.zeros((2, 128, 2 * quarter), BF16)
+
     barrier = pltpu.get_barrier_semaphore()
     for where in (across_x, across_y, across_core):
         pl.semaphore_signal(barrier, inc=1, device_id=where, device_id_type=MESH)
@@ -117,40 +122,42 @@
             if c < 2:
                 to_sides(c, z + s)
 
-    def in_order(act):
-        act(z)
-        for s in range(1, LINE):
-            pl.when(z >= s)(lambda s=s: act(z - s))
-            pl.when(z + s < LINE)(lambda s=s: act(z + s))
-
     def flatten(a, w, line):
         pair = blocks[a, w, pl.ds(2 * line, 2)].astype(F32).reshape(2 * rows, width)
         flat[a, pl.ds(pl.multiple_of(2 * rows * line, 16), 2 * rows), :] = pair.astype(BF16)
 
-    def share(a):
+    def share(a, w):
+        at = slice(w * second, w * second + window)
         mine = pl.ds(pl.multiple_of(dp * quarter, 128), quarter)
         other = pl.ds(pl.multiple_of((2 * y + 1 - core) * quarter, 128), quarter)
-        half[a, :, :quarter] = flat[a, :, mine]
-        half[a, :, quarter:] = flat[a, :, other]
+        half[a, at, :quarter] = flat[a, :, mine]
+        half[a, at, quarter:] = flat[a, :, other]
 
     def part(j):
         return pl.ds(pl.multiple_of(j * chunk, 16), chunk)
 
-    def forward(j):
+    def forward(w, j):
         for m in range(2):
-            pre[m, j] = contract(weights[m, part(j), :], flat[0], 1, 1)
-
-    def backward(j):
-        dhid[...] = contract(weights[2, part(j), :], flat[1], 1, 1)
+            pre[w, m, j] = contract(weights[m, part(j), :], flat[0], 1, 1)
+
+    pieces = ((0, 0, quarter), (1, quarter, window))
+
+    def backward(w, j):
+        dhid = contract(weights[2, part(j), :], flat[1], 1, 1)
+        for k, lo, hi in pieces:
+            acc[k, :chunk, : hi - lo] = dhid[:, lo:hi]
 
         def strip(i, _):
             at = pl.ds(pl.multiple_of(i * 16, 16), 16)
-            gate, up, part_hid = pre[0, j, at, :], pre[1, j, at, :], dhid[at, :]
-            sig = jax.nn.sigmoid(gate)
-            act = gate * sig
-            post[2, j, at, :] = (act * up).astype(BF16)
-            post[0, j, at, :] = (part_hid * up * sig * (1.0 + gate * (1.0 - sig))).astype(BF16)
-            post[1, j, at, :] = (part_hid * act).astype(BF16)
+            for k, lo, hi in pieces:
+                gate, up = pre[w, 0, j, at, lo:hi], pre[w, 1, j, at, lo:hi]
+                part_hid = acc[k, at, : hi - lo]
+                to = slice(w * second + lo, w * second + hi)
+                sig = jax.nn.sigmoid(gate)
+                act = gate * sig
+                post[2, j, at, to] = (act * up).astype(BF16)
+                post[0, j, at, to] = (part_hid * up * sig * (1.0 + gate * (1.0 - sig))).astype(BF16)
+                post[1, j, at, to] = (part_hid * act).astype(BF16)
             return 0
 
         lax.fori_loop(0, chunk // 16, strip, 0, unroll=5)
@@ -174,10 +181,10 @@
         flatten(0, 0, line)
     loads[0].wait()
     loads[1].wait()
-    forward(0)
+    forward(0, 0)
     step(1, 2)
     step(2, 2)
-    forward(1)
+    forward(0, 1)
     step(1, 3)
     step(2, 3)
 
@@ -197,24 +204,41 @@
 
         flatten(1, 0, line)
 
-    in_order(relay)
+    def relay_step(s):
+        pl.when(z >= s)(lambda: relay(z - s))
+        if s > 0:
+            pl.when(z + s < LINE)(lambda: relay(z + s))
+
+    relay_step(0)
+    relay_step(1)
+    share(0, 0)
+    for line in range(LINE):
+        @pl.when(line != z)
+        def _():
+            arrived(0, 1, 2 * line + x)
+
+        flatten(0, 1, line)
+    forward(1, 0)
+    relay_step(2)
+    forward(1, 1)
+    relay_step(3)
     arrived(1, 1, 2 * far + x)
     relay_far.start()
-    share(0)
-    share(1)
+    share(0, 1)
+    share(1, 0)
     loads[2].wait()
 
-    @pl.loop(0, n_chunks)
-    def _(j):
-        backward(j)
+    pl.loop(0, n_chunks)(lambda j: backward(0, j))
 
     for m in range(2):
-        turned[m] = post[m].reshape(hid, window).T
+        turned[m] = post[m, :, :, :window].reshape(hid, window).T
     for n in range(2):
         cols = slice(n * 2 * quarter, (n + 1) * 2 * quarter)
         total = contract(turned[0], weights[0, :, cols], 1, 0)
         total += contract(turned[1], weights[1, :, cols], 1, 0)
-        gi[:, :, cols] = total.reshape(2 * LINE, rows, 2 * quarter)
+        total = total.reshape(LINE, 2, rows, 2 * quarter)
+        gi[:, :, cols] = lax.select(x == 0, total[:, 0], total[:, 1])
+        gi_send[:, :, cols] = lax.select(x == 0, total[:, 1], total[:, 0]).astype(BF16)
 
     def gi_x(line):
         return pltpu.make_async_remote_copy(
@@ -231,38 +255,25 @@
         )
 
     for d in (2, 1, 3, 0):
-        line = (z + d) % LINE
-        gi_send[line] = gi[2 * line + 1 - x].astype(BF16)
-        gi_x(line).start()
-
-    @pl.loop(0, n_chunks)
-    def _(j):
-        for m, a in ((0, 0), (1, 0), (2, 1)):
-            acc[m, part(j), :] = contract(post[m, j], half[a], 1, 0)
-
+        gi_x((z + d) % LINE).start()
+
+    for line in range(LINE):
+        @pl.when(line != far)
+        def _():
+            arrived(1, 1, 2 * line + x)
+
+        arrived(1, 1, 2 * line + 1 - x)
+        flatten(1, 1, line)
+    share(1, 1)
+    backward(1, 0)
     for d in (2, 1, 3):
         line = (z + d) % LINE
         gi_x(line).wait_recv()
-        zs[d - 1] = (gi[2 * line + x] + gi_recv[line].astype(F32)).astype(BF16)
+        zs[d - 1] = (gi[line] + gi_recv[line].astype(F32)).astype(BF16)
         gi_z(d).start()
     gi_x(z).wait_recv()
 
-    for line in range(LINE):
-        @pl.when(line != z)
-        def _():
-            arrived(0, 1, 2 * line + x)
-
-        flatten(0, 1, line)
-    share(0)
-    pl.loop(0, n_chunks)(forward)
-    for line in range(LINE):
-        @pl.when(line != far)
-        def _():
-            arrived(1, 1, 2 * line + x)
-
-        arrived(1, 1, 2 * line + 1 - x)
-        flatten(1, 1, line)
-    share(1)
+    backward(1, 1)
 
     def dw_copy(m, j):
         return pltpu.make_async_remote_copy(
@@ -273,14 +284,13 @@
 
     @pl.loop(0, n_chunks)
     def _(j):
-        backward(j)
         for m, a in ((0, 0), (1, 0), (2, 1)):
-            total = acc[m, part(j), :] + contract(post[m, j], half[a], 1, 0)
-            acc[m, part(j), :] = total
+            total = contract(post[m, j], half[a], 1, 0)
+            acc[m, part(j), :] = total[:, :quarter]
             post[m, j, :, :quarter] = total[:, quarter:].astype(BF16)
             dw_copy(m, j).start()
 
-    total = gi[tp] + gi_recv[z].astype(F32)
+    total = gi[z] + gi_recv[z].astype(F32)
     for d in range(1, LINE):
         gi_z(d).wait_recv()
         total += zr[d - 1].astype(F32)
@@ -292,14 +302,14 @@
 
     def write(m, j):
         return pltpu.make_async_copy(
-            acc.at[m, part(j), pl.ds(0, quarter)], outs[m].at[part(j), :], out_sem.at[m, j]
+            acc.at[m, part(j), :], outs[m].at[part(j), :], out_sem.at[m, j]
         )
 
     @pl.loop(0, n_chunks)
     def _(j):
         for m in range(3):
             dw_copy(m, j).wait_recv()
-            acc[m, part(j), pl.ds(0, quarter)] += dw_recv[m, j].astype(F32)
+            acc[m, part(j), :] += dw_recv[m, j].astype(F32)
             write(m, j).start()
 
     gi_done.wait()
@@ -342,6 +352,7 @@
     chunk = hid // chunks
     window = 2 * LINE * rows
     quarter = width // 4
+    both = pl.cdiv(window, 128) * 128 + window
     dma = pltpu.SemaphoreType.DMA
     anywhere = pl.BlockSpec(memory_space=pl.ANY)
     outs = pl.pallas_call(
@@ -358,14 +369,13 @@
             pltpu.VMEM((2, 2, 2 * LINE, rows, width), BF16),
             pltpu.VMEM((3, hid, width), BF16),
             pltpu.VMEM((2, window, width), BF16),
-            pltpu.VMEM((2, window, width // 2), BF16),
+            pltpu.VMEM((2, both, width // 2), BF16),
             pltpu.VMEM((2, window, hid), BF16),
-            pltpu.VMEM((2, chunks, chunk, window), F32),
-            pltpu.VMEM((3, chunks, chunk, window), BF16),
-            pltpu.VMEM((chunk, window), F32),
-            pltpu.VMEM((3, hid, width // 2), F32),
+            pltpu.VMEM((2, 2, chunks, chunk, window), F32),
+            pltpu.VMEM((3, chunks, chunk, both), BF16),
+            pltpu.VMEM((3, hid, quarter), F32),
             pltpu.VMEM((3, chunks, chunk, quarter), BF16),
-            pltpu.VMEM((2 * LINE, rows, width), F32),
+            pltpu.VMEM((LINE, rows, width), F32),
             pltpu.VMEM((LINE, rows, width), BF16),
             pltpu.VMEM((LINE, rows, width), BF16),
             pltpu.VMEM((LINE - 1, rows, width), BF16),

time: 107 us -> 107 us (level)
  no operation moved by 1% of the time
where the time goes in v4:
time: 107 us
  Pallas kernels  101 us (94%)
  other arithmetic  4.89 us (5%)
    pallas_call x1, Pallas kernels, fused(): pl.pallas_call(kernel, out_shape=(jax.ShapeDtypeStruct((rows, width), BF1...  101 us
    div x1, other arithmetic, fused(): outs[3] / replicas  2.91 us

profile of v4, /device:TPU:0, one launch (start us, length us, event | category | flops | bytes accessed | tf_op | source)
XLA Modules:
  0.0 107.3 jit_solution(11971252349542924293)
XLA Ops:
  0.6 101.1 %shard_map.84 = (bf16[72,1536]{1,0:T(8,128)(2,1)}, f32[1120,384]{1,0:T(8,128)}, f32[1120,384]{1,0:T(8,128)}, f32[1120,384]{1,0:T(8,128)}) custom-call(bf16[72,1536]{1,0:T(8,128)(2,1)} %normed.1, bf16[72,1536]{1,0:T(8,128)(2,1)} %out_grad.1, bf16[1120,1536]{1,0:T(8,128)(2,1)} %bitcast.6, bf16[1120,1536]{1,0:T(8,128)(2,1)} %bitcast.7, bf16[1120,1536]{1,0:T(8,128)(2,1)} %down_w.1), custom_call_target="tpu_custom_call" | custom-call | flops 21799895040 | bytes 10321920 | tf_op jit(solution)/shard_map/pallas_call | solution.py:358
  101.7 0.0 copy-start
  101.7 0.0 copy-start.1
  101.7 2.9 %broadcast_multiply_fusion = f32[1120,384]{1,0:T(8,128)} fusion(f32[1120,384]{1,0:T(8,128)} %get-tuple-element.11), kind=kLoop, calls=%fused_computation.2 | loop fusion | flops 430080 | bytes 3440640 | tf_op jit(solution)/shard_map/div | solution.py:404
  104.6 0.0 copy-done
  104.6 0.0 copy-done.1
  104.6 0.0 copy-start.2
  104.6 2.0 %multiply_bitcast_fusion = (f32[384,1120]{0,1:T(8,128)}, f32[384,1120]{0,1:T(8,128)}) fusion(f32[1120,384]{1,0:T(8,128)S(1)} %copy-done.1, f32[1120,384]{1,0:T(8,128)S(1)} %copy-done), kind=kLoop, calls=%fused_computation | loop fusion | flops 860160 | bytes 6881280 | tf_op jit(solution)/shard_map/div | solution.py:404
  106.6 0.0 copy-done.2
  106.6 0.7 copy.10
Async XLA Ops:
  101.7 2.9 %copy-start = (f32[1120,384]{1,0:T(8,128)S(1)}, f32[1120,384]{1,0:T(8,128)}, u32[]{:S(2)}) copy-start(f32[1120,384]{1,0:T(8,128)} %get-tuple-element.9) | copy-start | bytes 5160964
  101.7 2.9 %copy-start.1 = (f32[1120,384]{1,0:T(8,128)S(1)}, f32[1120,384]{1,0:T(8,128)}, u32[]{:S(2)}) copy-start(f32[1120,384]{1,0:T(8,128)} %get-tuple-element.10) | copy-start | bytes 5160964
  104.6 2.0 %copy-start.2 = (bf16[72,1536]{1,0:T(8,128)(2,1)S(1)}, bf16[72,1536]{1,0:T(8,128)(2,1)}, u32[]{:S(2)}) copy-start(bf16[72,1536]{1,0:T(8,128)(2,1)} %get-tuple-element.18) | copy-start | bytes 663556

commit v5 on v4

--- a/solution.py
+++ b/solution.py
@@ -171,22 +171,19 @@
     own[1].wait()
     first(1)
     step(0, 2)
-    arrived(0, 1, 2 * z + 1 - x)
-    first(2)
     step(0, 3)
     step(1, 1)
-    step(2, 1)
+    arrived(0, 1, 2 * z + 1 - x)
     for line in range(LINE):
         arrived(0, 0, 2 * line + 1 - x)
         flatten(0, 0, line)
     loads[0].wait()
     loads[1].wait()
+    step(1, 2)
+    first(2)
     forward(0, 0)
-    step(1, 2)
-    step(2, 2)
+    step(1, 3)
     forward(0, 1)
-    step(1, 3)
-    step(2, 3)
 
     far = (z + 2) % LINE
 
@@ -211,52 +208,70 @@
 
     relay_step(0)
     relay_step(1)
+    step(2, 1)
+    relay_step(2)
+    relay_step(3)
+    step(2, 2)
     share(0, 0)
-    for line in range(LINE):
-        @pl.when(line != z)
-        def _():
-            arrived(0, 1, 2 * line + x)
-
-        flatten(0, 1, line)
-    forward(1, 0)
-    relay_step(2)
-    forward(1, 1)
-    relay_step(3)
+    share(1, 0)
+    loads[2].wait()
+
+    pl.loop(0, n_chunks)(lambda j: backward(0, j))
+    step(2, 3)
     arrived(1, 1, 2 * far + x)
     relay_far.start()
-    share(0, 1)
-    share(1, 0)
-    loads[2].wait()
-
-    pl.loop(0, n_chunks)(lambda j: backward(0, j))
 
     for m in range(2):
         turned[m] = post[m, :, :, :window].reshape(hid, window).T
+    def columns(n):
+        return slice(n * 2 * quarter, (n + 1) * 2 * quarter)
+
+    def gi_x(n, line):
+        cols = pl.ds(n * 2 * quarter, 2 * quarter)
+        return pltpu.make_async_remote_copy(
+            src_ref=gi_send.at[line, :, cols], dst_ref=gi_recv.at[line, :, cols],
+            send_sem=gxs_sem.at[n, line], recv_sem=gxr_sem.at[n, line],
+            device_id=across_x, device_id_type=MESH,
+        )
+
+    def gi_z(n, d):
+        cols = pl.ds(n * 2 * quarter, 2 * quarter)
+        return pltpu.make_async_remote_copy(
+            src_ref=zs.at[d - 1, :, cols], dst_ref=zr.at[d - 1, :, cols],
+            send_sem=gzs_sem.at[n, d - 1], recv_sem=gzr_sem.at[n, d - 1],
+            device_id={"tensor": 2 * ((z + d) % LINE) + x}, device_id_type=MESH,
+        )
+
     for n in range(2):
-        cols = slice(n * 2 * quarter, (n + 1) * 2 * quarter)
+        cols = columns(n)
         total = contract(turned[0], weights[0, :, cols], 1, 0)
         total += contract(turned[1], weights[1, :, cols], 1, 0)
         total = total.reshape(LINE, 2, rows, 2 * quarter)
         gi[:, :, cols] = lax.select(x == 0, total[:, 0], total[:, 1])
         gi_send[:, :, cols] = lax.select(x == 0, total[:, 1], total[:, 0]).astype(BF16)
-
-    def gi_x(line):
-        return pltpu.make_async_remote_copy(
-            src_ref=gi_send.at[line], dst_ref=gi_recv.at[line],
-            send_sem=gxs_sem.at[line], recv_sem=gxr_sem.at[line],
-            device_id=across_x, device_id_type=MESH,
-        )
-
-    def gi_z(d):
-        return pltpu.make_async_remote_copy(
-            src_ref=zs.at[d - 1], dst_ref=zr.at[d - 1],
-            send_sem=gzs_sem.at[d - 1], recv_sem=gzr_sem.at[d - 1],
-            device_id={"tensor": 2 * ((z + d) % LINE) + x}, device_id_type=MESH,
-        )
-
-    for d in (2, 1, 3, 0):
-        gi_x((z + d) % LINE).start()
-
+        for d in (2, 1, 3, 0):
+            gi_x(n, (z + d) % LINE).start()
+
+    def pass_on(n):
+        cols = columns(n)
+        for d in (2, 1, 3):
+            line = (z + d) % LINE
+            gi_x(n, line).wait_recv()
+            zs[d - 1, :, cols] = (gi[line, :, cols] + gi_recv[line, :, cols].astype(F32)).astype(BF16)
+            gi_z(n, d).start()
+        gi_x(n, z).wait_recv()
+
+    for line in range(LINE):
+        @pl.when(line != z)
+        def _():
+            arrived(0, 1, 2 * line + x)
+
+        flatten(0, 1, line)
+    share(0, 1)
+    forward(1, 0)
+    pass_on(0)
+    forward(1, 1)
+    pass_on(1)
     for line in range(LINE):
         @pl.when(line != far)
         def _():
@@ -266,13 +281,6 @@
         flatten(1, 1, line)
     share(1, 1)
     backward(1, 0)
-    for d in (2, 1, 3):
-        line = (z + d) % LINE
-        gi_x(line).wait_recv()
-        zs[d - 1] = (gi[line] + gi_recv[line].astype(F32)).astype(BF16)
-        gi_z(d).start()
-    gi_x(z).wait_recv()
-
     backward(1, 1)
 
     def dw_copy(m, j):
@@ -292,7 +300,8 @@
 
     total = gi[z] + gi_recv[z].astype(F32)
     for d in range(1, LINE):
-        gi_z(d).wait_recv()
+        for n in range(2):
+            gi_z(n, d).wait_recv()
         total += zr[d - 1].astype(F32)
     gi_out[...] = total.astype(BF16)
     gi_done = pltpu.make_async_copy(gi_out, grad_in, local_sem.at[0])
@@ -321,7 +330,8 @@
             write(m, j).wait()
 
     for line in range(LINE):
-        gi_x(line).wait_send()
+        for n in range(2):
+            gi_x(n, line).wait_send()
 
         @pl.when(line != far)
         def _():
@@ -342,7 +352,8 @@
     relay_x.wait_send()
     relay_far.wait_send()
     for d in range(1, LINE):
-        gi_z(d).wait_send()
+        for n in range(2):
+            gi_z(n, d).wait_send()
 
 
 def fused(normed, out_grad, gate_weight, up_weight, down_weight):
@@ -388,10 +399,10 @@
             dma((2, LINE)),
             dma((3, chunks)),
             dma((3, chunks)),
-            dma((LINE,)),
-            dma((LINE,)),
-            dma((LINE - 1,)),
-            dma((LINE - 1,)),
+            dma((2, LINE)),
+            dma((2, LINE)),
+            dma((2, LINE - 1)),
+            dma((2, LINE - 1)),
         ],
         compiler_params=pltpu.CompilerParams(
             collective_id=0, has_side_effects=True, vmem_limit_bytes=63 * 2**20

time: 107 us -> 107 us (level)
  no operation moved by 1% of the time
where the time goes in v5:
time: 107 us; the launch traced here: 106 us
  Pallas kernels  100 us (93%)
  other arithmetic  4.89 us (5%)
    pallas_call x1, Pallas kernels, fused(): pl.pallas_call(kernel, out_shape=(jax.ShapeDtypeStruct((rows, width), BF1...  100 us
    div x1, other arithmetic, fused(): outs[3] / replicas  2.91 us

profile of v5, /device:TPU:0, one launch (start us, length us, event | category | flops | bytes accessed | tf_op | source)
XLA Modules:
  0.0 106.4 jit_solution(1012031777871030210)
XLA Ops:
  0.6 100.2 %shard_map.84 = (bf16[72,1536]{1,0:T(8,128)(2,1)}, f32[1120,384]{1,0:T(8,128)}, f32[1120,384]{1,0:T(8,128)}, f32[1120,384]{1,0:T(8,128)}) custom-call(bf16[72,1536]{1,0:T(8,128)(2,1)} %normed.1, bf16[72,1536]{1,0:T(8,128)(2,1)} %out_grad.1, bf16[1120,1536]{1,0:T(8,128)(2,1)} %bitcast.6, bf16[1120,1536]{1,0:T(8,128)(2,1)} %bitcast.7, bf16[1120,1536]{1,0:T(8,128)(2,1)} %down_w.1), custom_call_target="tpu_custom_call" | custom-call | flops 21799895040 | bytes 10321920 | tf_op jit(solution)/shard_map/pallas_call | solution.py:369
  100.8 0.0 copy-start
  100.8 0.0 copy-start.1
  100.8 2.9 %broadcast_multiply_fusion = f32[1120,384]{1,0:T(8,128)} fusion(f32[1120,384]{1,0:T(8,128)} %get-tuple-element.11), kind=kLoop, calls=%fused_computation.2 | loop fusion | flops 430080 | bytes 3440640 | tf_op jit(solution)/shard_map/div | solution.py:415
  103.7 0.0 copy-done
  103.7 0.0 copy-done.1
  103.8 0.0 copy-start.2
  103.8 2.0 %multiply_bitcast_fusion = (f32[384,1120]{0,1:T(8,128)}, f32[384,1120]{0,1:T(8,128)}) fusion(f32[1120,384]{1,0:T(8,128)S(1)} %copy-done.1, f32[1120,384]{1,0:T(8,128)S(1)} %copy-done), kind=kLoop, calls=%fused_computation | loop fusion | flops 860160 | bytes 6881280 | tf_op jit(solution)/shard_map/div | solution.py:415
  105.7 0.0 copy-done.2
  105.7 0.7 copy.10
Async XLA Ops:
  100.8 2.9 %copy-start = (f32[1120,384]{1,0:T(8,128)S(1)}, f32[1120,384]{1,0:T(8,128)}, u32[]{:S(2)}) copy-start(f32[1120,384]{1,0:T(8,128)} %get-tuple-element.9) | copy-start | bytes 5160964
  100.8 2.9 %copy-start.1 = (f32[1120,384]{1,0:T(8,128)S(1)}, f32[1120,384]{1,0:T(8,128)}, u32[]{:S(2)}) copy-start(f32[1120,384]{1,0:T(8,128)} %get-tuple-element.10) | copy-start | bytes 5160964
  103.8 2.0 %copy-start.2 = (bf16[72,1536]{1,0:T(8,128)(2,1)S(1)}, bf16[72,1536]{1,0:T(8,128)(2,1)}, u32[]{:S(2)}) copy-start(bf16[72,1536]{1,0:T(8,128)(2,1)} %get-tuple-element.18) | copy-start | bytes 663556
